TPU v7x, 32 devices: a whole 2x2x4 slice. The times are simulated.
32 devices in a mesh: loop: 8 (over z, x), rep: 4 (over y, core).
Axes of the slice: x: 2, y: 2, z: 4, core: 2. Of those that a mesh axis runs over, the one named last changes fastest.
Arguments:
- features: bfloat16 [8192, 512], P(('loop', 'rep')), may hold values from -6 to 6
- adj_values: bfloat16 [8, 64, 4, 128, 128], P('loop', 'rep'), may hold values from -0.125 to 0.125
- adj_rows: int32 [8, 64, 4], P('loop', 'rep'), may hold values from 0 to 7
- slot_counts: int32 [8, 64], P('loop', 'rep'), may hold values from 1 to 4, as said below
- w_self: bfloat16 [512, 512], replicated, may hold values from -0.1875 to 0.1875
- w_neigh: bfloat16 [512, 512], replicated, may hold values from -0.1875 to 0.1875
- cotangent: bfloat16 [8192, 512], P(('loop', 'rep')), may hold values from -6 to 6
Outputs:
- activations: bfloat16 [8192, 512], P(('loop', 'rep'))
- grad_features: bfloat16 [8192, 512], P(('loop', 'rep'))
- grad_self: float32 [512, 512], replicated
- grad_neigh: float32 [512, 512], replicated
Inputs may be any that keep to these rules, and one draw needn't show every extreme that they name: `adj_rows`: A tile's rows lie in its own loop index's rows. Only the first slot_counts[l, c] slots of a column block are tiles of A; the others are ignored. The first column block of every device uses all 4 slots.
All inputs are finite; a program needn't handle non-finite values.
Results may differ from a plain program's by a relative error of at most 0.015.
Values may be sent and summed in bfloat16 or wider, within the bound.
A program may use at most 128 MiB of HBM per device.

v0:
```python
import math

import jax
import jax.numpy as jnp
from jax import lax
from jax.sharding import PartitionSpec as P


def body(features, adj_values, adj_rows, slot_counts, w_self, w_neigh, cotangent):
    rows_dev, width = features.shape
    tile = adj_values.shape[-1]
    nodes = rows_dev * lax.axis_size("loop") * lax.axis_size("rep")
    row_blocks = lax.axis_size("rep") * rows_dev // tile
    live = lax.broadcasted_iota(jnp.int32, adj_rows.shape[1:], 1) < slot_counts[0][:, None]
    tiles_live = adj_values[0] * live.astype(jnp.bfloat16)[:, :, None, None]
    block_rows = adj_rows[0]

    def tiles_for(count):
        blocks = count // tile
        return (tiles_live, block_rows)

    start_rows = jnp.zeros((row_blocks, tile, width), jnp.float32)
    piece = lax.all_gather(features, "loop", axis=0, tiled=True)
    blocks = piece.shape[0] // tile
    picked, targets = tiles_for(piece.shape[0])
    prod = jnp.einsum(
        "csij,cjd->csid",
        picked,
        piece.reshape(blocks, tile, width),
        preferred_element_type=jnp.float32,
    )
    partial_rows = start_rows.at[targets.reshape(-1)].add(prod.reshape(-1, tile, width))
    partial_flat = partial_rows.reshape(row_blocks * tile, width)
    agg = lax.psum_scatter(
        partial_flat.astype(jnp.bfloat16), "rep", scatter_dimension=0, tiled=True
    )
    z = jnp.dot(features, w_self, preferred_element_type=jnp.float32) + jnp.dot(
        agg, w_neigh, preferred_element_type=jnp.float32
    )
    activations = jax.nn.silu(z).astype(jnp.bfloat16)
    sig = jax.nn.sigmoid(z)
    dz = (cotangent.astype(jnp.float32) * sig * (1.0 + z * (1.0 - sig))).astype(jnp.bfloat16)
    over_rows = (((0,), (0,)), ((), ()))
    over_cols = (((1,), (1,)), ((), ()))
    dagg = lax.dot_general(dz, w_neigh, over_cols, preferred_element_type=jnp.float32).astype(
        jnp.bfloat16
    )
    dagg_rows = lax.all_gather(dagg, "rep", axis=0, tiled=True)
    dagg_blocks = dagg_rows.reshape(row_blocks, tile, width)
    count = lax.axis_size("loop") * rows_dev
    picked, targets = tiles_for(count)
    grads = dagg_blocks[targets]
    neighbour_part = lax.psum_scatter(
        jnp.einsum("csij,csid->cjd", picked, grads, preferred_element_type=jnp.float32)
        .reshape(count, width)
        .astype(jnp.bfloat16),
        "loop",
        scatter_dimension=0,
        tiled=True,
    ).astype(jnp.float32)
    local_self = lax.dot_general(features, dz, over_rows, preferred_element_type=jnp.float32)
    local_neigh = lax.dot_general(agg, dz, over_rows, preferred_element_type=jnp.float32)
    sums = lax.psum((local_self, local_neigh), ("loop", "rep"))
    factor = 1.0 / math.sqrt(nodes)
    self_part = lax.dot_general(dz, w_self, over_cols, preferred_element_type=jnp.float32)
    grad_features = (self_part + neighbour_part).astype(jnp.bfloat16)
    return (activations, grad_features, sums[0] * factor, sums[1] * factor)


def solution(mesh):
    placed = (
        P(("loop", "rep"), None),
        P("loop", "rep", None, None, None),
        P("loop", "rep", None),
        P("loop", "rep"),
        P(),
        P(),
        P(("loop", "rep"), None),
    )
    return jax.shard_map(
        body,
        mesh=mesh,
        in_specs=placed,
        out_specs=(P(("loop", "rep"), None), P(("loop", "rep"), None), P(), P()),
        check_vma=False,
    )
```

profile of v0, /device:TPU:1, one launch (start us, length us, event | category | flops | bytes accessed | tf_op | source)
XLA Modules:
  0.0 357.6 jit_solution(16931888446435736087)
XLA Ops:
  7.2 0.0 all-gather.3.cloned.1.call-start
  7.2 0.7 all-gather.3.cloned.1.call-update
  7.9 0.0 reduce-scatter.3.cloned.1.call-start
  8.0 0.8 copy.17
  8.7 0.1 reshape_squeeze.3
  8.8 0.7 fusion.4
  9.6 50.9 %all-gather.3.cloned.1.call-done = bf16[2048,512]{1,0:T(8,128)(2,1)} async-done(((bf16[256,512]{1,0:T(8,128)(2,1)}), bf16[2048,512]{1,0:T(8,128)(2,1)}) %all-gather.3.cloned.1.call-update) | async-done | bytes 2097168 | tf_op jit(solution)/shard_map/all_gather | solution.py:23
  60.4 10.4 %fusion = f32[16,4,128,512]{3,2,1,0:T(8,128)} fusion(bf16[16,128,512,1]{2,1,3,0:T(8,128)(2,1)} %bitcast.44, bf16[1,16,4,128,128]{4,3,2,1,0:T(8,128)(2,1)} %param.8, bf16[16,4]{1,0:T(8,128)(2,1)S(1)} %fusion.4), kind=kOutput, calls=%fused_computation.4 | convolution fusion | flops 1074790400 | bytes 20971648 | tf_op jit(solution)/shard_map/csij,cjd->csid/dot_general | solution.py:26
  70.8 0.2 broadcast_in_dim.2
  71.0 23.0 %scatter_fusion = f32[8,128,512]{2,1,0:T(8,128)S(1)} fusion(f32[8,128,512]{2,1,0:T(8,128)S(1)} %broadcast_in_dim.2, s32[64]{0:T(128)S(1)} %fusion.5, f32[64,128,512]{2,1,0:T(8,128)} %bitcast.40), kind=kCustom, calls=%fused_computation.1 | custom fusion | flops 4194304 | bytes 50331904 | tf_op jit(solution)/shard_map/scatter-add | solution.py:32
  94.1 1.1 convert_element_type.38
  95.2 0.0 reduce-scatter.3.cloned.1.call-update
  95.2 0.0 all-gather.5.cloned.1.call-start
  95.2 1.3 fusion.6
  96.6 23.3 %reduce-scatter.3.cloned.1.call-done = bf16[256,512]{1,0:T(8,128)(2,1)} async-done(((bf16[1024,512]{1,0:T(8,128)(2,1)}), bf16[256,512]{1,0:T(8,128)(2,1)}) %reduce-scatter.3.cloned.1.call-update) | async-done | bytes 262160 | tf_op jit(solution)/shard_map/reduce_scatter | solution.py:34
  119.9 2.2 multiply_convert_fusion
  122.0 1.0 convolution_convert_fusion
  123.1 0.0 all-reduce.3.cloned.1.call-start
  123.1 1.3 convolution_bitcast_fusion
  124.4 1.3 fusion.7
  125.8 0.0 reduce-scatter.5.cloned.1.call-start
  125.8 0.1 copy.18
  125.9 0.1 reshape.105
  126.0 14.3 %all-gather.5.cloned.1.call-done = bf16[1024,512]{1,0:T(8,128)(2,1)} async-done(((bf16[256,512]{1,0:T(8,128)(2,1)}), bf16[1024,512]{1,0:T(8,128)(2,1)}) %all-gather.5.cloned.1.call-update) | async-done | bytes 1048592 | tf_op jit(solution)/shard_map/all_gather | solution.py:48
  140.3 6.9 %gather_fusion = bf16[64,128,512]{2,1,0:T(8,128)(2,1)} fusion(bf16[8,128,512]{2,1,0:T(8,128)(2,1)} %bitcast.41, s32[1024]{0:T(1024)S(1)} %pad_clamp_fusion), kind=kCustom, calls=%fused_computation | custom fusion | bytes 16777472 | tf_op jit(solution)/shard_map/gather | solution.py:52
  147.2 6.6 %bitcast_convert_fusion = bf16[16,128,512]{2,1,0:T(8,128)(2,1)} fusion(bf16[16,4,128,512]{3,2,1,0:T(8,128)(2,1)} %bitcast.42, bf16[1,16,4,128,128]{4,3,2,1,0:T(8,128)(2,1)S(1)} %copy-done.1, bf16[16,4]{1,0:T(8,128)(2,1)S(1)} %fusion.4), kind=kOutput, calls=%fused_computation.2 | convolution fusion | flops 1075838976 | bytes 12583040 | tf_op jit(solution)/shard_map/csij,csid->cjd/dot_general | solution.py:54
  153.9 126.0 %all-reduce.3.cloned.1.call-done = (f32[512,512]{0,1:T(8,128)}, f32[512,512]{0,1:T(8,128)}) async-done(((f32[512,512]{0,1:T(8,128)}, f32[512,512]{0,1:T(8,128)}), (f32[512,512]{0,1:T(8,128)}, f32[512,512]{0,1:T(8,128)})) %all-reduce.3.cloned.1.call-update) | async-done | bytes 2097168 | tf_op jit(solution)/shard_map/psum | solution.py:63
  279.8 1.8 broadcast_multiply_fusion
  281.6 1.3 copy.21
  283.0 1.3 copy.22
  284.3 64.9 %reduce-scatter.5.cloned.1.call-done = bf16[256,512]{1,0:T(8,128)(2,1)} async-done(((bf16[2048,512]{1,0:T(8,128)(2,1)}), bf16[256,512]{1,0:T(8,128)(2,1)}) %reduce-scatter.5.cloned.1.call-update) | async-done | bytes 262160 | tf_op jit(solution)/shard_map/reduce_scatter | solution.py:53
  349.1 2.0 fusion.1
  (20 shorter events, 0.1 us)
Async XLA Ops:
  7.2 112.7 %copy-start = (bf16[512,512]{1,0:T(8,128)(2,1)S(1)}, bf16[512,512]{1,0:T(8,128)(2,1)}, u32[]{:S(2)}) copy-start(bf16[512,512]{1,0:T(8,128)(2,1)} %param.12) | copy-start | bytes 1572868
  7.2 53.3 %all-gather.3.cloned.1.call-start = ((), (), s32[]{:S(2)}) async-start(), calls=%async_computation.2 | async-start | bytes 2359296 | tf_op jit(solution)/shard_map/all_gather | solution.py:23
  7.9 111.9 %reduce-scatter.3.cloned.1.call-start = ((), (), s32[]{:S(2)}) async-start(), calls=%async_computation.3 | async-start | bytes 1310720 | tf_op jit(solution)/shard_map/reduce_scatter | solution.py:34
  94.0 1.2 copy-start.2
  94.0 25.8 %copy-start.6 = (bf16[256,512]{1,0:T(8,128)(2,1)S(1)}, bf16[256,512]{1,0:T(8,128)(2,1)}, u32[]{:S(2)}) copy-start(bf16[256,512]{1,0:T(8,128)(2,1)} %param.13) | copy-start | bytes 786436
  95.2 45.2 %all-gather.5.cloned.1.call-start = ((), (), s32[]{:S(2)}) async-start(), calls=%async_computation.4 | async-start | bytes 1310720 | tf_op jit(solution)/shard_map/all_gather | solution.py:48
  122.0 2.4 copy-start.4
  123.1 156.8 %all-reduce.3.cloned.1.call-start = ((), (), s32[]{:S(2)}) async-start(), calls=%async_computation.6 | async-start | bytes 4194304 | tf_op jit(solution)/shard_map/psum | solution.py:63
  124.4 1.4 copy-start.5
  125.8 223.4 %reduce-scatter.5.cloned.1.call-start = ((), (), s32[]{:S(2)}) async-start(), calls=%async_computation.5 | async-start | bytes 2359296 | tf_op jit(solution)/shard_map/reduce_scatter | solution.py:53
  140.3 6.9 %copy-start.1 = (bf16[1,16,4,128,128]{4,3,2,1,0:T(8,128)(2,1)S(1)}, bf16[1,16,4,128,128]{4,3,2,1,0:T(8,128)(2,1)}, u32[]{:S(2)}) copy-start(bf16[1,16,4,128,128]{4,3,2,1,0:T(8,128)(2,1)} %param.8) | copy-start | bytes 6291460
  281.6 67.5 %copy-start.3 = (bf16[512,512]{1,0:T(8,128)(2,1)S(1)}, bf16[512,512]{1,0:T(8,128)(2,1)}, u32[]{:S(2)}) copy-start(bf16[512,512]{1,0:T(8,128)(2,1)} %param.11) | copy-start | bytes 1572868
Sparse Core Ops, SparseCore 0:
  10.1 50.2 all-gather.2
  95.3 24.5 reduce-scatter.2
  123.2 17.0 all-gather.4
  147.2 132.5 all-reduce.2
  283.2 65.8 reduce-scatter.4
where the time goes:
time: 361 us; the launch traced here: 358 us
  waiting for transfers between devices  280 us (78%)
  other arithmetic  26.6 us (7%)
  matrix products  26.1 us (7%)
  between operations  13.9 us (4%)
  local copies, waits for them, and re-layouts  10.8 us (3%)
    psum x1, waiting for transfers between devices, body(): sums = lax.psum((local_self, local_neigh), ('loop', 'rep'))  126 us
    reduce_scatter x1, waiting for transfers between devices, body(): lax.psum_scatter(jnp.einsum('csij,csid->cjd', picked, grads, preferred_el...  64.9 us
    all_gather x1, waiting for transfers between devices, body(): piece = lax.all_gather(features, 'loop', axis=0, tiled=True)  50.9 us
    reduce_scatter x1, waiting for transfers between devices, body(): lax.psum_scatter(partial_flat.astype(jnp.bfloat16), 'rep', scatter_dimens...  23.3 us
    scatter-add x1, other arithmetic, body(): start_rows.at[targets.reshape(-1)].add(prod.reshape(-1, tile, width))  23 us
    all_gather x1, waiting for transfers between devices, body(): dagg_rows = lax.all_gather(dagg, 'rep', axis=0, tiled=True)  14.3 us
    dot_general x1, matrix products, body(): jnp.einsum('csij,cjd->csid', picked, piece.reshape(blocks, tile, width),...  10.4 us
  transfers between devices with their start and end apart: 5, of which 5 were waited for; matrix products, arithmetic and copies ran while one was open for 7% of the time, Pallas kernels for 0%

commit v1 on v0

--- a/solution.py
+++ b/solution.py
@@ -1,9 +1,374 @@
+import functools
 import math
 
 import jax
 import jax.numpy as jnp
 from jax import lax
+from jax.experimental import pallas as pl
+from jax.experimental.pallas import tpu as pltpu
 from jax.sharding import PartitionSpec as P
+
+MESH = pl.DeviceIdType.MESH
+SLAB_LIMIT = 8 * 1024 * 1024
+OVER_ROWS = (((0,), (0,)), ((), ()))
+OVER_COLS = (((1,), (1,)), ((), ()))
+
+
+def mm(a, b, dims=(((1,), (0,)), ((), ()))):
+    return lax.dot_general(a, b, dims, preferred_element_type=jnp.float32)
+
+
+def loop(low, high, step):
+    def one(k, carry):
+        step(k)
+        return carry
+
+    lax.fori_loop(low, high, one, 0)
+
+
+def kernel(
+    nl, nr, scale,
+    f_ref, adj_ref, rows_ref, cnt_ref, ws_ref, wn_ref, ct_ref,
+    act_ref, gf_ref, gs_ref, gn_ref,
+    dense, gat, acc, b1s, b1r, b2s, b2r, zf, fa, dz, dall,
+    g1s, g1r, g32, g2s, g2r, g3f, g3s, g3r, gfin,
+    f1s, f1r, f2s, f2r, total,
+    sem_a, sem_x, rec_a, sem_b1, rec_b1, sem_b2, rec_b2, sem_d, sem_ds, rec_d,
+    sem_g1, rec_g1, sem_g2, rec_g2, sem_g3, rec_g3, sem_g4, rec_g4, sem_g5, rec_g5,
+    sem_g6, rec_g6, sem_f1, rec_f1, sem_f2, rec_f2,
+):
+    nz, ny = nl // 2, nr // 2
+    rows, width = f_ref.shape
+    tile = adj_ref.shape[-1]
+    slots = adj_ref.shape[2]
+    part = width // ny
+    bf16, f32 = jnp.bfloat16, jnp.float32
+    li, ri = lax.axis_index("loop"), lax.axis_index("rep")
+    z, x = lax.div(li, 2), lax.rem(li, 2)
+    y, c = lax.div(ri, 2), lax.rem(ri, 2)
+    xp = z * 2 + 1 - x
+    sib = y * 2 + 1 - c
+
+    def zat(k):
+        return lax.rem(z + k, nz)
+
+    def yat(k):
+        return lax.rem(y + k, ny)
+
+    def lat(k):
+        return lax.rem(li + k, nl)
+
+    def rowsof(r):
+        return pl.ds(pl.multiple_of(r * rows, rows), rows)
+
+    def send(src, dst, s, r, lo, re):
+        return pltpu.make_async_remote_copy(
+            src_ref=src, dst_ref=dst, send_sem=s, recv_sem=r,
+            device_id=(lo, re), device_id_type=MESH,
+        )
+
+    barrier = pltpu.get_barrier_semaphore()
+    for k in range(1, nl):
+        pl.semaphore_signal(barrier, inc=1, device_id=(lat(k), ri), device_id_type=MESH)
+    for k in range(1, ny):
+        pl.semaphore_signal(
+            barrier, inc=1, device_id=(li, yat(k) * 2 + c), device_id_type=MESH
+        )
+    pl.semaphore_signal(barrier, inc=1, device_id=(li, sib), device_id_type=MESH)
+    pl.semaphore_wait(barrier, nl - 1 + ny)
+
+    def send_a(k):
+        return send(f_ref, gat.at[li], sem_a.at[k], rec_a.at[li], zat(k) * 2 + x, ri)
+
+    def send_x0():
+        return send(f_ref, gat.at[li], sem_x.at[0], rec_a.at[li], xp, ri)
+
+    def send_x(k):
+        j = zat(k) * 2 + x
+        return send(gat.at[j], gat.at[j], sem_x.at[k], rec_a.at[j], xp, ri)
+
+    def got_a(j):
+        send(gat.at[j], gat.at[j], sem_x.at[0], rec_a.at[j], xp, ri).wait_recv()
+
+    send_x0().start()
+    for k in range(1, nz):
+        send_a(k).start()
+
+    per = rows // tile
+    row_blocks = nr * per
+
+    def build(col):
+        j, h = lax.div(col, per), lax.rem(col, per)
+        cols = pl.ds(pl.multiple_of(h * tile, tile), tile)
+        count = cnt_ref[0, col]
+        places = [
+            jnp.where(s < count, rows_ref[0, col, s], -1) for s in range(slots)
+        ]
+
+        for b in range(row_blocks):
+            block = jnp.zeros((tile, tile), f32)
+            for s in range(slots):
+                keep = jnp.where(places[s] == b, 1.0, 0.0).astype(f32)
+                block = block + adj_ref[0, col, s].astype(f32) * keep
+            dense[j, b * tile : (b + 1) * tile, cols] = block.astype(bf16)
+
+    loop(0, nl * per, build)
+    zf[...] = mm(f_ref[...], ws_ref[...])
+    fa[0] = f_ref[...]
+    acc[...] = mm(dense[li], f_ref[...])
+
+    def column(k):
+        j = zat(k) * 2 + x
+        got_a(j)
+        send_x(k).start()
+        acc[...] += mm(dense[j], gat[j])
+
+    loop(1, nz, column)
+
+    def across(k):
+        j = zat(k) * 2 + 1 - x
+        got_a(j)
+        acc[...] += mm(dense[j], gat[j])
+
+    loop(0, nz, across)
+
+    def send_b1(k):
+        return send(b1s.at[k], b1r.at[k], sem_b1.at[k], rec_b1.at[k], li, sib)
+
+    def send_b2(k):
+        return send(
+            b2s.at[k - 1], b2r.at[k - 1], sem_b2.at[k - 1], rec_b2.at[k - 1],
+            li, yat(k) * 2 + c,
+        )
+
+    order = list(range(1, ny)) + [0]
+    for k in order:
+        b1s[k] = acc[rowsof(yat(k) * 2 + 1 - c), :].astype(bf16)
+        send_b1(k).start()
+    for k in order:
+        send_b1(k).wait_recv()
+        summed = acc[rowsof(yat(k) * 2 + c), :] + b1r[k].astype(f32)
+        if k:
+            b2s[k - 1] = summed.astype(bf16)
+            send_b2(k).start()
+        else:
+            total[...] = summed
+    for k in range(1, ny):
+        send_b2(k).wait_recv()
+        total[...] += b2r[k - 1].astype(f32)
+    fa[1] = total[...].astype(bf16)
+
+    zz = zf[...] + mm(fa[1], wn_ref[...])
+    sig = jax.nn.sigmoid(zz)
+    act_ref[...] = (zz * sig).astype(bf16)
+    dz[...] = (ct_ref[...].astype(f32) * sig * (1.0 + zz * (1.0 - sig))).astype(bf16)
+    dall[rowsof(ri), :] = mm(dz[...], wn_ref[...], OVER_COLS).astype(bf16)
+
+    def send_d(k):
+        at = dall.at[rowsof(ri)]
+        return send(at, at, sem_d.at[k - 1], rec_d.at[ri], li, yat(k) * 2 + c)
+
+    def send_ds(k):
+        r = yat(k) * 2 + c
+        at = dall.at[rowsof(r)]
+        return send(at, at, sem_ds.at[k], rec_d.at[r], li, sib)
+
+    def got_d(r):
+        at = dall.at[rowsof(r)]
+        send(at, at, sem_ds.at[0], rec_d.at[r], li, sib).wait_recv()
+
+    for k in range(1, ny):
+        send_d(k).start()
+    send_ds(0).start()
+
+    send_g1 = send(g1s, g1r, sem_g1, rec_g1, li, sib)
+    g1s[...] = mm(fa[1 - c], dz[...], OVER_ROWS).astype(bf16)
+    send_g1.start()
+    g32[...] = mm(fa[c], dz[...], OVER_ROWS)
+    for k in range(1, ny):
+        got_d(yat(k) * 2 + c)
+        send_ds(k).start()
+    send_g1.wait_recv()
+    g32[...] += g1r[...].astype(f32)
+
+    def partof(yy):
+        return pl.ds(pl.multiple_of(yy * part, part), part)
+
+    def send_g2(k):
+        return send(
+            g2s.at[k - 1], g2r.at[k - 1], sem_g2.at[k - 1], rec_g2.at[k - 1],
+            li, yat(k) * 2 + c,
+        )
+
+    for k in range(1, ny):
+        g2s[k - 1] = g32[partof(yat(k)), :].astype(bf16)
+        send_g2(k).start()
+    for k in range(ny):
+        got_d(yat(k) * 2 + 1 - c)
+
+    def send_f1(k):
+        return send(f1s.at[k], f1r.at[k], sem_f1.at[k], rec_f1.at[k], xp, ri)
+
+    def send_f2(k):
+        return send(
+            f2s.at[k - 1], f2r.at[k - 1], sem_f2.at[k - 1], rec_f2.at[k - 1],
+            zat(k) * 2 + x, ri,
+        )
+
+    def away(i):
+        k = lax.rem(i, nz)
+        f1s[k] = mm(dense[zat(k) * 2 + 1 - x], dall[...], OVER_ROWS).astype(bf16)
+        send_f1(k).start()
+
+    loop(1, nz + 1, away)
+
+    def send_g3(k):
+        return send(
+            g3s.at[lat(k)], g3r.at[k - 1], sem_g3.at[k - 1], rec_g3.at[k - 1], lat(k), ri
+        )
+
+    mine = g32[partof(y), :]
+    for k in range(1, ny):
+        send_g2(k).wait_recv()
+        mine = mine + g2r[k - 1].astype(f32)
+    g3f[...] = mine.reshape(g3f.shape)
+    g3s[...] = g3f[...].astype(bf16)
+    for k in range(1, nl):
+        send_g3(k).start()
+
+    def home(k):
+        value = mm(dense[zat(k) * 2 + x], dall[...], OVER_ROWS)
+        send_f1(k).wait_recv()
+        f2s[k - 1] = (value + f1r[k].astype(f32)).astype(bf16)
+        send_f2(k).start()
+
+    loop(1, nz, home)
+
+    def send_g4(k):
+        at = gfin.at[c, y, li]
+        return send(at, at, sem_g4.at[k - 1], rec_g4.at[li], lat(k), ri)
+
+    small = g3f[li]
+    for k in range(1, nl):
+        send_g3(k).wait_recv()
+        small = small + g3r[k - 1].astype(f32)
+    gfin[c, y, li] = small.astype(bf16)
+    for k in range(1, nl):
+        send_g4(k).start()
+    total[...] = mm(dz[...], ws_ref[...], OVER_COLS) + mm(
+        dense[li], dall[...], OVER_ROWS
+    )
+    send_f1(0).wait_recv()
+    total[...] += f1r[0].astype(f32)
+    for k in range(1, nl):
+        at = gfin.at[c, y, lat(k)]
+        send(at, at, sem_g4.at[0], rec_g4.at[lat(k)], lat(k), ri).wait_recv()
+
+    def send_g5(k):
+        at = gfin.at[c, y]
+        return send(at, at, sem_g5.at[k - 1], rec_g5.at[y], li, yat(k) * 2 + c)
+
+    def send_g6(k):
+        at = gfin.at[c, yat(k)]
+        return send(at, at, sem_g6.at[k], rec_g6.at[yat(k)], li, sib)
+
+    for k in range(1, ny):
+        send_g5(k).start()
+    send_g6(0).start()
+    for k in range(1, ny):
+        at = gfin.at[c, yat(k)]
+        send(at, at, sem_g5.at[0], rec_g5.at[yat(k)], li, yat(k) * 2 + c).wait_recv()
+        send_g6(k).start()
+    for k in range(1, nz):
+        send_f2(k).wait_recv()
+        total[...] += f2r[k - 1].astype(f32)
+    gf_ref[...] = total[...].astype(bf16)
+    for k in range(ny):
+        at = gfin.at[1 - c, yat(k)]
+        send(at, at, sem_g6.at[0], rec_g6.at[yat(k)], li, sib).wait_recv()
+    gs_ref[...] = gfin[0].reshape(width, width).astype(f32) * scale
+    gn_ref[...] = gfin[1].reshape(width, width).astype(f32) * scale
+
+    send_x0().wait_send()
+    for k in range(1, nz):
+        send_a(k).wait_send()
+        send_x(k).wait_send()
+        send_f2(k).wait_send()
+    for k in range(nz):
+        send_f1(k).wait_send()
+    for k in range(ny):
+        send_b1(k).wait_send()
+        send_ds(k).wait_send()
+        send_g6(k).wait_send()
+    for k in range(1, ny):
+        send_b2(k).wait_send()
+        send_d(k).wait_send()
+        send_g2(k).wait_send()
+        send_g5(k).wait_send()
+    send_g1.wait_send()
+    for k in range(1, nl):
+        send_g3(k).wait_send()
+        send_g4(k).wait_send()
+
+
+def fused(nl, nr, features, adj_values, adj_rows, slot_counts, w_self, w_neigh, cotangent):
+    rows, width = features.shape
+    bf16, f32 = jnp.bfloat16, jnp.float32
+    nz, ny = nl // 2, nr // 2
+    part = width // ny
+    q = part // nl
+    scale = 1.0 / math.sqrt(rows * nl * nr)
+    vm = pl.BlockSpec(memory_space=pltpu.VMEM)
+    sm = pl.BlockSpec(memory_space=pltpu.SMEM)
+
+    def buf(*shape):
+        return pltpu.VMEM(shape, bf16)
+
+    def wide(*shape):
+        return pltpu.VMEM(shape, f32)
+
+    def dma(*shape):
+        return pltpu.SemaphoreType.DMA(shape)
+
+    out = pl.pallas_call(
+        functools.partial(kernel, nl, nr, scale),
+        out_shape=(
+            jax.ShapeDtypeStruct((rows, width), bf16),
+            jax.ShapeDtypeStruct((rows, width), bf16),
+            jax.ShapeDtypeStruct((width, width), f32),
+            jax.ShapeDtypeStruct((width, width), f32),
+        ),
+        in_specs=[vm, vm, sm, sm, vm, vm, vm],
+        out_specs=(vm, vm, vm, vm),
+        scratch_shapes=[
+            buf(nl, nr * rows, rows), buf(nl, rows, width), wide(nr * rows, width),
+            buf(ny, rows, width), buf(ny, rows, width),
+            buf(ny - 1, rows, width), buf(ny - 1, rows, width),
+            wide(rows, width), buf(2, rows, width), buf(rows, width), buf(nr * rows, width),
+            buf(width, width), buf(width, width), wide(width, width),
+            buf(ny - 1, part, width), buf(ny - 1, part, width),
+            wide(nl, q, width), buf(nl, q, width), buf(nl - 1, q, width),
+            buf(2, ny, nl, q, width),
+            buf(nz, rows, width), buf(nz, rows, width),
+            buf(nz - 1, rows, width), buf(nz - 1, rows, width), wide(rows, width),
+            dma(nz), dma(nz), dma(nl), dma(ny), dma(ny), dma(ny - 1), dma(ny - 1),
+            dma(ny - 1), dma(ny), dma(nr),
+            pltpu.SemaphoreType.DMA, pltpu.SemaphoreType.DMA, dma(ny - 1), dma(ny - 1),
+            dma(nl - 1), dma(nl - 1), dma(nl - 1), dma(nl), dma(ny - 1), dma(ny),
+            dma(ny), dma(ny), dma(nz), dma(nz), dma(nz - 1), dma(nz - 1),
+        ],
+        compiler_params=pltpu.CompilerParams(
+            collective_id=0, has_side_effects=True, vmem_limit_bytes=48 * 1024 * 1024
+        ),
+    )(features, adj_values, adj_rows, slot_counts, w_self, w_neigh, cotangent)
+    return tuple(out)
+
+
+def choose(nl, nr, features, *rest):
+    rows = features.shape[0]
+    if nl * nr * rows * rows * 2 > SLAB_LIMIT:
+        return body(features, *rest)
+    return fused(nl, nr, features, *rest)
 
 
 def body(features, adj_values, adj_rows, slot_counts, w_self, w_neigh, cotangent):
@@ -78,7 +443,7 @@
         P(("loop", "rep"), None),
     )
     return jax.shard_map(
-        body,
+        functools.partial(choose, mesh.shape["loop"], mesh.shape["rep"]),
         mesh=mesh,
         in_specs=placed,
         out_specs=(P(("loop", "rep"), None), P(("loop", "rep"), None), P(), P()),

time: 361 us -> 122 us (0.34)
  waiting for transfers between devices: 280 us -> 0 us
  Pallas kernels: 0 us -> 112 us
  other arithmetic: 26.6 us -> 0 us
  matrix products: 26.1 us -> 0 us
  between operations: 13.9 us -> 0.65 us
    psum x1 -> x0, waiting for transfers between devices: 126 us -> none  [body(): sums = lax.psum((local_self, local_neigh), ('loop', 'rep'))]
    pallas_call x0 -> x1, Pallas kernels: none -> 112 us  [fused(): pl.pallas_call(functools.partial(kernel, nl, nr, scale), out_shape=(jax.S...]
    reduce_scatter x2 -> x0, waiting for transfers between devices: 88.1 us -> none  [the longest x1 64.9 us: body(): lax.psum_scatter(jnp.einsum('csij,csid->cjd', picked, grads, preferred_el...]
    all_gather x2 -> x0, waiting for transfers between devices: 65.2 us -> none  [the longest x1 50.9 us: body(): piece = lax.all_gather(features, 'loop', axis=0, tiled=True)]
    dot_general x8 -> x0, matrix products: 26.1 us -> none  [the longest x1 10.4 us: body(): jnp.einsum('csij,cjd->csid', picked, piece.reshape(blocks, tile, width),...]
    scatter-add x1 -> x0, other arithmetic: 23 us -> none  [body(): start_rows.at[targets.reshape(-1)].add(prod.reshape(-1, tile, width))]
    gather x1 -> x0, local copies, waits for them, and re-layouts: 6.86 us -> none  [body(): grads = dagg_blocks[targets]]
    unnamed x17 -> x15, local copies, waits for them, and re-layouts: 3.41 us -> 8.74 us
  transfers between devices with their start and end apart: 5 -> 0, of which waited for: 5 -> 0; matrix products, arithmetic and copies ran while one was open for 7% -> 0% of each run, Pallas kernels for 0% -> 0%
where the time goes in v1:
time: 122 us; the launch traced here: 121 us
  Pallas kernels  112 us (92%)
  local copies, waits for them, and re-layouts  8.74 us (7%)
    pallas_call x1, Pallas kernels, fused(): pl.pallas_call(functools.partial(kernel, nl, nr, scale), out_shape=(jax.S...  112 us
    unnamed x15, local copies, waits for them, and re-layouts  8.74 us

profile of v1, /device:TPU:1, one launch (start us, length us, event | category | flops | bytes accessed | tf_op | source)
XLA Modules:
  0.0 121.1 jit_solution(6751401231835175048)
XLA Ops:
  0.6 0.8 copy.11.rows_ref
  1.4 0.0 copy-start
  1.4 1.0 copy-done
  2.4 0.0 copy-start.1
  2.4 1.0 copy-done.1
  3.5 0.0 copy-start.2
  3.5 0.9 copy-done.2
  4.4 0.0 copy-start.3
  4.4 0.9 copy-done.3
  5.4 0.0 copy-start.4
  5.4 0.7 copy-done.4
  6.0 111.8 %shard_map.102 = (bf16[256,512]{1,0:T(8,128)(2,1)S(1)}, bf16[256,512]{1,0:T(8,128)(2,1)S(1)}, f32[512,512]{1,0:T(8,128)S(1)}, f32[512,512]{1,0:T(8,128)S(1)}) custom-call(bf16[256,512]{1,0:T(8,128)(2,1)S(1)} %copy-done.2, bf16[1,16,4,128,128]{4,3,2,1,0:T(8,128)(2,1)} %adj_ref.1, s32[1,16,4]{2,1,0:T(8,128)S(1)} %copy.11.rows_ref, s32[1,16]{1,0:T(1,128)S(1)} %copy-done.4, ...), custom_call_target="tpu_custom_call" | custom-call | tf_op jit(solution)/shard_map/pallas_call | solution.py:333
  117.8 0.7 copy.16
  118.5 0.7 copy.17
  119.2 1.0 copy.18
  120.2 1.0 copy.19
Async XLA Ops:
  1.4 1.0 copy-start
  2.4 1.0 copy-start.1
  3.5 0.9 copy-start.2
  4.4 0.9 copy-start.3
  5.4 0.7 copy-start.4

commit v2 on v1

--- a/solution.py
+++ b/solution.py
@@ -9,6 +9,7 @@
 from jax.sharding import PartitionSpec as P
 
 MESH = pl.DeviceIdType.MESH
+HALVES = 2
 SLAB_LIMIT = 8 * 1024 * 1024
 OVER_ROWS = (((0,), (0,)), ((), ()))
 OVER_COLS = (((1,), (1,)), ((), ()))
@@ -27,20 +28,22 @@
 
 
 def kernel(
-    nl, nr, scale,
-    f_ref, adj_ref, rows_ref, cnt_ref, ws_ref, wn_ref, ct_ref,
+    nl, nr,
+    f_hbm, adj_hbm, rows_ref, cnt_ref, ws_hbm, wn_hbm, ct_hbm,
     act_ref, gf_ref, gs_ref, gn_ref,
+    f_ref, adj_ref, ws_ref, wn_ref, ct_ref, sem_in,
     dense, gat, acc, b1s, b1r, b2s, b2r, zf, fa, dz, dall,
     g1s, g1r, g32, g2s, g2r, g3f, g3s, g3r, gfin,
-    f1s, f1r, f2s, f2r, total,
-    sem_a, sem_x, rec_a, sem_b1, rec_b1, sem_b2, rec_b2, sem_d, sem_ds, rec_d,
+    f1s, f1r, ups, upr, dns, dnr, value, total,
+    sem_au, sem_ad, sem_x, rec_a, sem_b1, rec_b1, sem_b2, rec_b2, sem_d, sem_ds, rec_d,
     sem_g1, rec_g1, sem_g2, rec_g2, sem_g3, rec_g3, sem_g4, rec_g4, sem_g5, rec_g5,
-    sem_g6, rec_g6, sem_f1, rec_f1, sem_f2, rec_f2,
+    sem_g6, rec_g6, sem_f1, rec_f1, sem_up, rec_up, sem_dn, rec_dn,
 ):
     nz, ny = nl // 2, nr // 2
     rows, width = f_ref.shape
     tile = adj_ref.shape[-1]
     slots = adj_ref.shape[2]
+    half = rows // HALVES
     part = width // ny
     bf16, f32 = jnp.bfloat16, jnp.float32
     li, ri = lax.axis_index("loop"), lax.axis_index("rep")
@@ -48,6 +51,7 @@
     y, c = lax.div(ri, 2), lax.rem(ri, 2)
     xp = z * 2 + 1 - x
     sib = y * 2 + 1 - c
+    below, above = z > 0, z < nz - 1
 
     def zat(k):
         return lax.rem(z + k, nz)
@@ -75,25 +79,61 @@
             barrier, inc=1, device_id=(li, yat(k) * 2 + c), device_id_type=MESH
         )
     pl.semaphore_signal(barrier, inc=1, device_id=(li, sib), device_id_type=MESH)
+    loads = [
+        pltpu.make_async_copy(src, dst, sem_in.at[i])
+        for i, (src, dst) in enumerate(
+            ((f_hbm, f_ref), (adj_hbm, adj_ref), (ws_hbm, ws_ref), (wn_hbm, wn_ref), (ct_hbm, ct_ref))
+        )
+    ]
+    for load in loads:
+        load.start()
+    loads[0].wait()
     pl.semaphore_wait(barrier, nl - 1 + ny)
 
-    def send_a(k):
-        return send(f_ref, gat.at[li], sem_a.at[k], rec_a.at[li], zat(k) * 2 + x, ri)
-
-    def send_x0():
-        return send(f_ref, gat.at[li], sem_x.at[0], rec_a.at[li], xp, ri)
-
-    def send_x(k):
-        j = zat(k) * 2 + x
-        return send(gat.at[j], gat.at[j], sem_x.at[k], rec_a.at[j], xp, ri)
-
-    def got_a(j):
-        send(gat.at[j], gat.at[j], sem_x.at[0], rec_a.at[j], xp, ri).wait_recv()
-
-    send_x0().start()
-    for k in range(1, nz):
-        send_a(k).start()
-
+    def block(p, h):
+        at = pl.ds(h * half, half)
+        return gat.at[p * 2 + x, at, :]
+
+    def own(h):
+        return f_ref.at[pl.ds(h * half, half), :]
+
+    def send_x(p, h, src=None):
+        at = block(p, h)
+        return send(
+            at if src is None else src, at, sem_x.at[p, h], rec_a.at[p * 2 + x, h], xp, ri
+        )
+
+    def send_au(p, h, src=None):
+        at = block(p, h)
+        return send(
+            at if src is None else src, at, sem_au.at[p, h], rec_a.at[p * 2 + x, h],
+            (z + 1) * 2 + x, ri,
+        )
+
+    def send_ad(p, h, src=None):
+        at = block(p, h)
+        return send(
+            at if src is None else src, at, sem_ad.at[p, h], rec_a.at[p * 2 + x, h],
+            (z - 1) * 2 + x, ri,
+        )
+
+    def got_a(j, h):
+        at = gat.at[j, pl.ds(h * half, half), :]
+        send(at, at, sem_x.at[0, 0], rec_a.at[j, h], xp, ri).wait_recv()
+
+    for h in range(HALVES):
+        @pl.when(above)
+        def _():
+            send_au(z, h, own(h)).start()
+
+        @pl.when(below)
+        def _():
+            send_ad(z, h, own(h)).start()
+
+        send_x(z, h, own(h)).start()
+
+    for load in loads[1:]:
+        load.wait()
     per = rows // tile
     row_blocks = nr * per
 
@@ -102,32 +142,53 @@
         cols = pl.ds(pl.multiple_of(h * tile, tile), tile)
         count = cnt_ref[0, col]
         places = [
-            jnp.where(s < count, rows_ref[0, col, s], -1) for s in range(slots)
+            jnp.where(s < count, rows_ref[0, s, col], -1) for s in range(slots)
         ]
 
         for b in range(row_blocks):
-            block = jnp.zeros((tile, tile), f32)
+            summed = jnp.zeros((tile, tile), f32)
             for s in range(slots):
                 keep = jnp.where(places[s] == b, 1.0, 0.0).astype(f32)
-                block = block + adj_ref[0, col, s].astype(f32) * keep
-            dense[j, b * tile : (b + 1) * tile, cols] = block.astype(bf16)
+                summed = summed + adj_ref[0, col, s].astype(f32) * keep
+            dense[j, b * tile : (b + 1) * tile, cols] = summed.astype(bf16)
 
     loop(0, nl * per, build)
     zf[...] = mm(f_ref[...], ws_ref[...])
     fa[0] = f_ref[...]
     acc[...] = mm(dense[li], f_ref[...])
 
+    for k in range(1, nz):
+        for h in range(HALVES):
+            @pl.when(z >= k)
+            def _():
+                got_a((z - k) * 2 + x, h)
+
+                @pl.when(above)
+                def _():
+                    send_au(z - k, h).start()
+
+                send_x(z - k, h).start()
+
+            @pl.when(z + k < nz)
+            def _():
+                got_a((z + k) * 2 + x, h)
+
+                @pl.when(below)
+                def _():
+                    send_ad(z + k, h).start()
+
+                send_x(z + k, h).start()
+
     def column(k):
         j = zat(k) * 2 + x
-        got_a(j)
-        send_x(k).start()
         acc[...] += mm(dense[j], gat[j])
 
     loop(1, nz, column)
 
     def across(k):
         j = zat(k) * 2 + 1 - x
-        got_a(j)
+        for h in range(HALVES):
+            got_a(j, h)
         acc[...] += mm(dense[j], gat[j])
 
     loop(0, nz, across)
@@ -206,21 +267,51 @@
     for k in range(ny):
         got_d(yat(k) * 2 + 1 - c)
 
-    def send_f1(k):
-        return send(f1s.at[k], f1r.at[k], sem_f1.at[k], rec_f1.at[k], xp, ri)
-
-    def send_f2(k):
-        return send(
-            f2s.at[k - 1], f2r.at[k - 1], sem_f2.at[k - 1], rec_f2.at[k - 1],
-            zat(k) * 2 + x, ri,
-        )
-
-    def away(i):
-        k = lax.rem(i, nz)
-        f1s[k] = mm(dense[zat(k) * 2 + 1 - x], dall[...], OVER_ROWS).astype(bf16)
-        send_f1(k).start()
-
-    loop(1, nz + 1, away)
+    def send_f1(d, h):
+        return send(f1s.at[d, h], f1r.at[d, h], sem_f1.at[d, h], rec_f1.at[d, h], xp, ri)
+
+    def send_up(d, h):
+        return send(
+            ups.at[d, h], upr.at[d, h], sem_up.at[d, h], rec_up.at[d, h], (z + 1) * 2 + x, ri
+        )
+
+    def send_dn(d, h):
+        return send(
+            dns.at[d, h], dnr.at[d, h], sem_dn.at[d, h], rec_dn.at[d, h], (z - 1) * 2 + x, ri
+        )
+
+    def away(d):
+        product = mm(dense[d * 2 + 1 - x], dall[...], OVER_ROWS).astype(bf16)
+        f1s[d] = product.reshape(HALVES, half, width)
+        for h in range(HALVES):
+            send_f1(d, h).start()
+
+    def home(d, move, out, come, more):
+        product = mm(dense[d * 2 + x], dall[...], OVER_ROWS)
+        value[...] = product.reshape(HALVES, half, width)
+        for h in range(HALVES):
+            send_f1(d, h).wait_recv()
+            value[h] += f1r[d, h].astype(f32)
+
+            @pl.when(more)
+            def _():
+                move(d, h).wait_recv()
+                value[h] += come[d, h].astype(f32)
+
+            out[d, h] = value[h].astype(bf16)
+            move(d, h).start()
+
+    def sides(k, up, down):
+        @pl.when(z + k < nz)
+        def _():
+            up(z + k)
+
+        @pl.when(z >= k)
+        def _():
+            down(z - k)
+
+    for k in range(nz - 1, nz // 2 - 1, -1):
+        sides(k, away, away)
 
     def send_g3(k):
         return send(
@@ -236,13 +327,18 @@
     for k in range(1, nl):
         send_g3(k).start()
 
-    def home(k):
-        value = mm(dense[zat(k) * 2 + x], dall[...], OVER_ROWS)
-        send_f1(k).wait_recv()
-        f2s[k - 1] = (value + f1r[k].astype(f32)).astype(bf16)
-        send_f2(k).start()
-
-    loop(1, nz, home)
+    for k in range(nz // 2 - 1, 0, -1):
+        sides(k, away, away)
+    away(z)
+
+    def home_up(d):
+        home(d, send_up, ups, upr, below)
+
+    def home_down(d):
+        home(d, send_dn, dns, dnr, above)
+
+    for k in range(nz - 1, nz // 2 - 1, -1):
+        sides(k, home_up, home_down)
 
     def send_g4(k):
         at = gfin.at[c, y, li]
@@ -255,11 +351,11 @@
     gfin[c, y, li] = small.astype(bf16)
     for k in range(1, nl):
         send_g4(k).start()
+    for k in range(nz // 2 - 1, 0, -1):
+        sides(k, home_up, home_down)
     total[...] = mm(dz[...], ws_ref[...], OVER_COLS) + mm(
         dense[li], dall[...], OVER_ROWS
     )
-    send_f1(0).wait_recv()
-    total[...] += f1r[0].astype(f32)
     for k in range(1, nl):
         at = gfin.at[c, y, lat(k)]
         send(at, at, sem_g4.at[0], rec_g4.at[lat(k)], lat(k), ri).wait_recv()
@@ -279,23 +375,49 @@
         at = gfin.at[c, yat(k)]
         send(at, at, sem_g5.at[0], rec_g5.at[yat(k)], li, yat(k) * 2 + c).wait_recv()
         send_g6(k).start()
-    for k in range(1, nz):
-        send_f2(k).wait_recv()
-        total[...] += f2r[k - 1].astype(f32)
+    for h in range(HALVES):
+        at = slice(h * half, (h + 1) * half)
+        send_f1(z, h).wait_recv()
+        total[at] += f1r[z, h].astype(f32)
+
+        @pl.when(below)
+        def _():
+            send_up(z, h).wait_recv()
+            total[at] += upr[z, h].astype(f32)
+
+        @pl.when(above)
+        def _():
+            send_dn(z, h).wait_recv()
+            total[at] += dnr[z, h].astype(f32)
+
     gf_ref[...] = total[...].astype(bf16)
     for k in range(ny):
         at = gfin.at[1 - c, yat(k)]
         send(at, at, sem_g6.at[0], rec_g6.at[yat(k)], li, sib).wait_recv()
-    gs_ref[...] = gfin[0].reshape(width, width).astype(f32) * scale
-    gn_ref[...] = gfin[1].reshape(width, width).astype(f32) * scale
-
-    send_x0().wait_send()
-    for k in range(1, nz):
-        send_a(k).wait_send()
-        send_x(k).wait_send()
-        send_f2(k).wait_send()
-    for k in range(nz):
-        send_f1(k).wait_send()
+    gs_ref[...] = gfin[0].reshape(width, width)
+    gn_ref[...] = gfin[1].reshape(width, width)
+
+    for h in range(HALVES):
+        for p in range(nz):
+            send_x(p, h).wait_send()
+            send_f1(p, h).wait_send()
+
+            @pl.when(above & (p <= z))
+            def _():
+                send_au(p, h).wait_send()
+
+            @pl.when(below & (p >= z))
+            def _():
+                send_ad(p, h).wait_send()
+
+            @pl.when(p > z)
+            def _():
+                send_up(p, h).wait_send()
+
+            @pl.when(p < z)
+            def _():
+                send_dn(p, h).wait_send()
+
     for k in range(ny):
         send_b1(k).wait_send()
         send_ds(k).wait_send()
@@ -320,6 +442,8 @@
     scale = 1.0 / math.sqrt(rows * nl * nr)
     vm = pl.BlockSpec(memory_space=pltpu.VMEM)
     sm = pl.BlockSpec(memory_space=pltpu.SMEM)
+    hbm = pl.BlockSpec(memory_space=pl.ANY)
+    half = rows // HALVES
 
     def buf(*shape):
         return pltpu.VMEM(shape, bf16)
@@ -331,16 +455,18 @@
         return pltpu.SemaphoreType.DMA(shape)
 
     out = pl.pallas_call(
-        functools.partial(kernel, nl, nr, scale),
+        functools.partial(kernel, nl, nr),
         out_shape=(
             jax.ShapeDtypeStruct((rows, width), bf16),
             jax.ShapeDtypeStruct((rows, width), bf16),
-            jax.ShapeDtypeStruct((width, width), f32),
-            jax.ShapeDtypeStruct((width, width), f32),
+            jax.ShapeDtypeStruct((width, width), bf16),
+            jax.ShapeDtypeStruct((width, width), bf16),
         ),
-        in_specs=[vm, vm, sm, sm, vm, vm, vm],
+        in_specs=[hbm, hbm, sm, sm, hbm, hbm, hbm],
         out_specs=(vm, vm, vm, vm),
         scratch_shapes=[
+            buf(rows, width), buf(*adj_values.shape), buf(width, width), buf(width, width),
+            buf(rows, width), dma(5),
             buf(nl, nr * rows, rows), buf(nl, rows, width), wide(nr * rows, width),
             buf(ny, rows, width), buf(ny, rows, width),
             buf(ny - 1, rows, width), buf(ny - 1, rows, width),
@@ -349,19 +475,19 @@
             buf(ny - 1, part, width), buf(ny - 1, part, width),
             wide(nl, q, width), buf(nl, q, width), buf(nl - 1, q, width),
             buf(2, ny, nl, q, width),
-            buf(nz, rows, width), buf(nz, rows, width),
-            buf(nz - 1, rows, width), buf(nz - 1, rows, width), wide(rows, width),
-            dma(nz), dma(nz), dma(nl), dma(ny), dma(ny), dma(ny - 1), dma(ny - 1),
+            *[buf(nz, HALVES, half, width) for _ in range(6)],
+            wide(HALVES, half, width), wide(rows, width),
+            dma(nz, HALVES), dma(nz, HALVES), dma(nz, HALVES), dma(nl, HALVES), dma(ny), dma(ny), dma(ny - 1), dma(ny - 1),
             dma(ny - 1), dma(ny), dma(nr),
             pltpu.SemaphoreType.DMA, pltpu.SemaphoreType.DMA, dma(ny - 1), dma(ny - 1),
             dma(nl - 1), dma(nl - 1), dma(nl - 1), dma(nl), dma(ny - 1), dma(ny),
-            dma(ny), dma(ny), dma(nz), dma(nz), dma(nz - 1), dma(nz - 1),
+            dma(ny), dma(ny), *[dma(nz, HALVES) for _ in range(6)],
         ],
         compiler_params=pltpu.CompilerParams(
-            collective_id=0, has_side_effects=True, vmem_limit_bytes=48 * 1024 * 1024
+            collective_id=0, has_side_effects=True, vmem_limit_bytes=60 * 1024 * 1024
         ),
-    )(features, adj_values, adj_rows, slot_counts, w_self, w_neigh, cotangent)
-    return tuple(out)
+    )(features, adj_values, jnp.swapaxes(adj_rows, 1, 2), slot_counts, w_self, w_neigh, cotangent)
+    return (out[0], out[1], out[2].astype(f32) * scale, out[3].astype(f32) * scale)
 
 
 def choose(nl, nr, features, *rest):

time: 122 us -> 95.9 us (0.79)
  Pallas kernels: 112 us -> 90.8 us
  local copies, waits for them, and re-layouts: 8.74 us -> 1.41 us
  other arithmetic: 0 us -> 2.87 us
    pallas_call x1, Pallas kernels: 112 us -> 90.8 us  [fused(): pl.pallas_call(functools.partial(kernel, nl, nr), out_shape=(jax.ShapeDty...]
    unnamed x15 -> x6, local copies, waits for them, and re-layouts: 8.74 us -> 1.41 us
    mul x0 -> x1, other arithmetic: none -> 2.87 us  [fused(): out[3].astype(f32) * scale]
where the time goes in v2:
time: 95.9 us; the launch traced here: 95.8 us
  Pallas kernels  90.8 us (95%)
  other arithmetic  2.87 us (3%)
  local copies, waits for them, and re-layouts  1.41 us (1%)
    pallas_call x1, Pallas kernels, fused(): pl.pallas_call(functools.partial(kernel, nl, nr), out_shape=(jax.ShapeDty...  90.8 us
    mul x1, other arithmetic, fused(): out[3].astype(f32) * scale  2.87 us

profile of v2, /device:TPU:1, one launch (start us, length us, event | category | flops | bytes accessed | tf_op | source)
XLA Modules:
  0.0 95.8 jit_solution(12875165495303605211)
XLA Ops:
  0.6 90.8 %shard_map.102 = (bf16[256,512]{1,0:T(8,128)(2,1)}, bf16[256,512]{1,0:T(8,128)(2,1)}, bf16[512,512]{1,0:T(8,128)(2,1)}, bf16[512,512]{1,0:T(8,128)(2,1)}) custom-call(bf16[256,512]{1,0:T(8,128)(2,1)} %f_hbm.1, bf16[1,16,4,128,128]{4,3,2,1,0:T(8,128)(2,1)} %adj_hbm.1, s32[1,4,16]{2,1,0:T(4,128)} %bitcast.1, s32[1,16]{1,0:T(1,128)} %cnt_ref.1, ...), custom_call_target="tpu_custom_call" | custom-call | tf_op jit(solution)/shard_map/pallas_call | solution.py:457
  91.5 0.0 copy-start.1
  91.5 0.0 copy-start
  91.5 2.9 %convert_multiply_fusion = (f32[512,512]{1,0:T(8,128)}, f32[512,512]{1,0:T(8,128)}) fusion(bf16[512,512]{1,0:T(8,128)(2,1)} %get-tuple-element.11, bf16[512,512]{1,0:T(8,128)(2,1)} %get-tuple-element.10), kind=kLoop, calls=%fused_computation | loop fusion | flops 1048576 | bytes 3145728 | tf_op jit(solution)/shard_map/mul | solution.py:490
  94.3 0.0 copy-done.1
  94.3 0.7 copy.13
  95.1 0.0 copy-done
  95.1 0.7 copy.14
Async XLA Ops:
  91.5 2.9 %copy-start.1 = (bf16[256,512]{1,0:T(8,128)(2,1)S(1)}, bf16[256,512]{1,0:T(8,128)(2,1)}, u32[]{:S(2)}) copy-start(bf16[256,512]{1,0:T(8,128)(2,1)} %get-tuple-element.18) | copy-start | bytes 786436
  91.5 3.6 %copy-start = (bf16[256,512]{1,0:T(8,128)(2,1)S(1)}, bf16[256,512]{1,0:T(8,128)(2,1)}, u32[]{:S(2)}) copy-start(bf16[256,512]{1,0:T(8,128)(2,1)} %get-tuple-element.19) | copy-start | bytes 786436

commit v3 on v2

--- a/solution.py
+++ b/solution.py
@@ -356,25 +356,32 @@
     total[...] = mm(dz[...], ws_ref[...], OVER_COLS) + mm(
         dense[li], dall[...], OVER_ROWS
     )
-    for k in range(1, nl):
-        at = gfin.at[c, y, lat(k)]
-        send(at, at, sem_g4.at[0], rec_g4.at[lat(k)], lat(k), ri).wait_recv()
-
-    def send_g5(k):
-        at = gfin.at[c, y]
-        return send(at, at, sem_g5.at[k - 1], rec_g5.at[y], li, yat(k) * 2 + c)
-
-    def send_g6(k):
-        at = gfin.at[c, yat(k)]
-        return send(at, at, sem_g6.at[k], rec_g6.at[yat(k)], li, sib)
-
-    for k in range(1, ny):
-        send_g5(k).start()
-    send_g6(0).start()
-    for k in range(1, ny):
-        at = gfin.at[c, yat(k)]
-        send(at, at, sem_g5.at[0], rec_g5.at[yat(k)], li, yat(k) * 2 + c).wait_recv()
-        send_g6(k).start()
+    def send_g5(k, p):
+        at = gfin.at[c, y, p]
+        return send(
+            at, at, sem_g5.at[k - 1, p], rec_g5.at[y, p], li, yat(k) * 2 + c
+        )
+
+    def send_g6(k, p):
+        at = gfin.at[c, yat(k), p]
+        return send(at, at, sem_g6.at[k, p], rec_g6.at[yat(k), p], li, sib)
+
+    for i in range(nl):
+        p = lat(i)
+        if i:
+            at = gfin.at[c, y, p]
+            send(at, at, sem_g4.at[0], rec_g4.at[p], p, ri).wait_recv()
+        for k in range(1, ny):
+            send_g5(k, p).start()
+        send_g6(0, p).start()
+    for k in range(1, ny):
+        for i in range(nl):
+            p = lat(i)
+            at = gfin.at[c, yat(k), p]
+            send(
+                at, at, sem_g5.at[0, p], rec_g5.at[yat(k), p], li, yat(k) * 2 + c
+            ).wait_recv()
+            send_g6(k, p).start()
     for h in range(HALVES):
         at = slice(h * half, (h + 1) * half)
         send_f1(z, h).wait_recv()
@@ -392,8 +399,9 @@
 
     gf_ref[...] = total[...].astype(bf16)
     for k in range(ny):
-        at = gfin.at[1 - c, yat(k)]
-        send(at, at, sem_g6.at[0], rec_g6.at[yat(k)], li, sib).wait_recv()
+        for p in range(nl):
+            at = gfin.at[1 - c, yat(k), p]
+            send(at, at, sem_g6.at[0, p], rec_g6.at[yat(k), p], li, sib).wait_recv()
     gs_ref[...] = gfin[0].reshape(width, width)
     gn_ref[...] = gfin[1].reshape(width, width)
 
@@ -421,12 +429,14 @@
     for k in range(ny):
         send_b1(k).wait_send()
         send_ds(k).wait_send()
-        send_g6(k).wait_send()
+        for p in range(nl):
+            send_g6(k, p).wait_send()
     for k in range(1, ny):
         send_b2(k).wait_send()
         send_d(k).wait_send()
         send_g2(k).wait_send()
-        send_g5(k).wait_send()
+        for p in range(nl):
+            send_g5(k, p).wait_send()
     send_g1.wait_send()
     for k in range(1, nl):
         send_g3(k).wait_send()
@@ -480,8 +490,8 @@
             dma(nz, HALVES), dma(nz, HALVES), dma(nz, HALVES), dma(nl, HALVES), dma(ny), dma(ny), dma(ny - 1), dma(ny - 1),
             dma(ny - 1), dma(ny), dma(nr),
             pltpu.SemaphoreType.DMA, pltpu.SemaphoreType.DMA, dma(ny - 1), dma(ny - 1),
-            dma(nl - 1), dma(nl - 1), dma(nl - 1), dma(nl), dma(ny - 1), dma(ny),
-            dma(ny), dma(ny), *[dma(nz, HALVES) for _ in range(6)],
+            dma(nl - 1), dma(nl - 1), dma(nl - 1), dma(nl), dma(ny - 1, nl), dma(ny, nl),
+            dma(ny, nl), dma(ny, nl), *[dma(nz, HALVES) for _ in range(6)],
         ],
         compiler_params=pltpu.CompilerParams(
             collective_id=0, has_side_effects=True, vmem_limit_bytes=60 * 1024 * 1024

time: 95.9 us -> 95.4 us (level)
  no operation moved by 1% of the time
where the time goes in v3:
time: 95.4 us; the launch traced here: 95.2 us
  Pallas kernels  90.3 us (95%)
  other arithmetic  2.87 us (3%)
  local copies, waits for them, and re-layouts  1.41 us (1%)
    pallas_call x1, Pallas kernels, fused(): pl.pallas_call(functools.partial(kernel, nl, nr), out_shape=(jax.ShapeDty...  90.3 us
    mul x1, other arithmetic, fused(): out[3].astype(f32) * scale  2.87 us

profile of v3, /device:TPU:1, one launch (start us, length us, event | category | flops | bytes accessed | tf_op | source)
XLA Modules:
  0.0 95.2 jit_solution(15507644130336629223)
XLA Ops:
  0.6 90.3 %shard_map.102 = (bf16[256,512]{1,0:T(8,128)(2,1)}, bf16[256,512]{1,0:T(8,128)(2,1)}, bf16[512,512]{1,0:T(8,128)(2,1)}, bf16[512,512]{1,0:T(8,128)(2,1)}) custom-call(bf16[256,512]{1,0:T(8,128)(2,1)} %f_hbm.1, bf16[1,16,4,128,128]{4,3,2,1,0:T(8,128)(2,1)} %adj_hbm.1, s32[1,4,16]{2,1,0:T(4,128)} %bitcast.1, s32[1,16]{1,0:T(1,128)} %cnt_ref.1, ...), custom_call_target="tpu_custom_call" | custom-call | tf_op jit(solution)/shard_map/pallas_call | solution.py:467
  90.9 0.0 copy-start.1
  90.9 0.0 copy-start
  90.9 2.9 %convert_multiply_fusion = (f32[512,512]{1,0:T(8,128)}, f32[512,512]{1,0:T(8,128)}) fusion(bf16[512,512]{1,0:T(8,128)(2,1)} %get-tuple-element.11, bf16[512,512]{1,0:T(8,128)(2,1)} %get-tuple-element.10), kind=kLoop, calls=%fused_computation | loop fusion | flops 1048576 | bytes 3145728 | tf_op jit(solution)/shard_map/mul | solution.py:500
  93.8 0.0 copy-done.1
  93.8 0.7 copy.13
  94.5 0.0 copy-done
  94.5 0.7 copy.14
Async XLA Ops:
  90.9 2.9 %copy-start.1 = (bf16[256,512]{1,0:T(8,128)(2,1)S(1)}, bf16[256,512]{1,0:T(8,128)(2,1)}, u32[]{:S(2)}) copy-start(bf16[256,512]{1,0:T(8,128)(2,1)} %get-tuple-element.18) | copy-start | bytes 786436
  90.9 3.6 %copy-start = (bf16[256,512]{1,0:T(8,128)(2,1)S(1)}, bf16[256,512]{1,0:T(8,128)(2,1)}, u32[]{:S(2)}) copy-start(bf16[256,512]{1,0:T(8,128)(2,1)} %get-tuple-element.19) | copy-start | bytes 786436
